TPU v7x, 128 devices: a whole 4x4x4 slice. The times are simulated.
128 devices in a mesh: ctx: 16 (over z, x), head: 2 (over y_hi), dp: 4 (over y_lo, core).
Axes of the slice: x: 4, y: 4 (y_hi: 2, y_lo: 2; y = y_hi * 2 + y_lo), z: 4, core: 2. Of those that a mesh axis runs over, the one named last changes fastest.
Arguments:
- queries: bfloat16 [4, 2048, 5120], P('dp', 'ctx', 'head'), may hold values from -200 to 200
- keys: bfloat16 [4, 16384, 1024], P('dp', 'ctx', 'head'), may hold values from -6 to 6
- start_block: int32 [4], P('dp'), may hold values from 0 to 224, as said below
- lengths: int32 [4], P('dp'), may hold values from 2048 to 16384, as said below
- gate_query: bfloat16 [8, 640, 128], P('head'), may hold values from -2 to 2
- gate_key: bfloat16 [8, 384, 128], P('head'), may hold values from -0.3125 to 0.3125
Outputs:
- grad_query: float32 [8, 640, 128], P('head')
- grad_key: float32 [8, 384, 128], P('head')
- block_loss: float32 [4, 8], P('dp', 'head')
Inputs may be any that keep to these rules, and one draw needn't show every extreme that they name: The span's 32 blocks lie inside the context: start_block + 32 <= 256. Every query token of the span lies before the sequence's length: lengths >= 64 * (start_block + 32).
All inputs are finite; a program needn't handle non-finite values.
Results may differ from a plain program's by a relative error of at most 0.0003.
Values may be sent and summed in bfloat16 or wider, within the bound.
No kernel may reach another device: no remote copies, remote signals or barrier semaphores. Data moves between devices by JAX's collectives and lax.ppermute only.
A program may use at most 320 MiB of HBM per device.

v0:
```python
import jax
import jax.numpy as jnp
from jax import lax
from jax.sharding import PartitionSpec as P

BLK = 64
GROUP = 5


NEG = -1e30
HIGH = lax.Precision.HIGHEST


def teacher_rows(rows, key_group, first_row, seq_length):
    row_count = rows.shape[0]
    ctx_len = key_group.shape[0]
    scores = jnp.einsum(
        "qhd,kd->hqk", rows, key_group, preferred_element_type=jnp.float32
    ) * rows.shape[2] ** (-0.5)
    query_pos = first_row + jnp.arange(row_count, dtype=jnp.int32)
    key_pos = jnp.arange(ctx_len, dtype=jnp.int32)
    visible = (key_pos[None, :] <= query_pos[:, None]) & (key_pos[None, :] < seq_length)
    masked = jnp.where(visible[None], scores, NEG)
    row_top = jnp.max(masked, axis=2, keepdims=True)
    weights = jnp.where(visible[None], jnp.exp(masked - row_top), 0.0)
    probs = weights / jnp.sum(weights, axis=2, keepdims=True)
    pooled = probs.reshape(GROUP, row_count // BLK, BLK, ctx_len // BLK, BLK).max(axis=(2, 4))
    return jnp.mean(pooled, axis=0)


def pool_queries(grouped):
    groups, row_count, width = grouped.shape
    return jnp.mean(
        grouped.astype(jnp.float32).reshape(groups, row_count // BLK, BLK, width), axis=2
    )


def pool_keys(grouped):
    groups, row_count, width = grouped.shape
    blocks = grouped.astype(jnp.float32).reshape(groups, row_count // BLK, BLK, width)
    return jnp.concatenate([blocks.max(axis=2), blocks.min(axis=2), blocks.mean(axis=2)], axis=2)


def gate_logits(pooled_q, pooled_k, weight_q, weight_k, q_blocks, k_blocks, seq_length):
    proj_q = jnp.einsum("gqc,gcd->gqd", pooled_q, weight_q.astype(jnp.float32), precision=HIGH)
    proj_k = jnp.einsum("gkc,gcd->gkd", pooled_k, weight_k.astype(jnp.float32), precision=HIGH)
    logits = jnp.einsum("gqd,gkd->gqk", proj_q, proj_k, precision=HIGH) * proj_q.shape[2] ** (-0.5)
    visible = (k_blocks[None, :] <= q_blocks[:, None]) & (k_blocks[None, :] * BLK < seq_length)
    masked = jnp.where(visible[None], logits, NEG)
    return (proj_q, proj_k, masked, visible)


def gate_grads(pooled_k, proj_q, proj_k, masked, visible, gate_top, gate_sum, target, blocks_q):
    gate_prob = jnp.where(visible[None], jnp.exp(masked - gate_top) / gate_sum, 0.0)
    log_gate = masked - gate_top - jnp.log(gate_sum)
    terms = jax.scipy.special.xlogy(target, target) - jnp.where(
        visible[None], target * log_gate, 0.0
    )
    kl_loss = jnp.sum(terms, axis=(1, 2)) / blocks_q
    slope = (gate_prob - target) / blocks_q
    scale_factor = proj_q.shape[2] ** (-0.5)
    slope_q = jnp.einsum("gqk,gkd->gqd", slope, proj_k, precision=HIGH) * scale_factor
    slope_k = jnp.einsum("gqk,gqd->gkd", slope, proj_q, precision=HIGH) * scale_factor
    grad_k = jnp.einsum("gkc,gkd->gcd", pooled_k, slope_k, precision=HIGH)
    return (kl_loss, slope_q, grad_k)


def per_device(queries, keys, start_block, lengths, gate_query, gate_key):
    groups = gate_query.shape[0]
    head_dim = keys.shape[2] // groups
    ctx_count = lax.axis_size("ctx")
    ctx_index = lax.axis_index("ctx")
    start_blk = start_block[0]
    seq_length = lengths[0]
    row_count = queries.shape[1]
    blocks_q = row_count * ctx_count // BLK
    whole_keys = lax.all_gather(keys, "ctx", axis=1, tiled=True)[0]
    ctx_len = whole_keys.shape[0]
    key_heads = whole_keys.reshape(ctx_len, groups, head_dim).transpose(1, 0, 2)
    query_heads = queries[0].reshape(row_count, groups, GROUP, head_dim).transpose(1, 0, 2, 3)
    first_row = start_blk * BLK + ctx_index * row_count

    def per_group(operands):
        return teacher_rows(operands[0], operands[1], first_row, seq_length)

    teacher = lax.map(per_group, (query_heads, key_heads))
    target = teacher / jnp.sum(teacher, axis=2, keepdims=True)
    pooled_q = pool_queries(
        queries[0].reshape(row_count, groups, GROUP * head_dim).transpose(1, 0, 2)
    )
    pooled_k = pool_keys(key_heads)
    q_blocks = (
        start_blk + ctx_index * (row_count // BLK) + jnp.arange(row_count // BLK, dtype=jnp.int32)
    )
    k_blocks = jnp.arange(ctx_len // BLK, dtype=jnp.int32)
    proj_q, proj_k, masked, visible = gate_logits(
        pooled_q, pooled_k, gate_query, gate_key, q_blocks, k_blocks, seq_length
    )
    gate_top = jnp.max(masked, axis=2, keepdims=True)
    gate_sum = jnp.sum(
        jnp.where(visible[None], jnp.exp(masked - gate_top), 0.0), axis=2, keepdims=True
    )
    kl_loss, slope_q, grad_k = gate_grads(
        pooled_k, proj_q, proj_k, masked, visible, gate_top, gate_sum, target, blocks_q
    )
    dp_count = lax.axis_size("dp")
    dp_index = lax.axis_index("dp")
    selector = (jnp.arange(dp_count, dtype=jnp.int32) == dp_index).astype(jnp.float32)
    loss_rows = selector[:, None] * kl_loss[None, :]
    grad_q = jnp.einsum("gqc,gqd->gcd", pooled_q, slope_q, precision=HIGH)
    grad_q, grad_k, loss_rows = lax.psum((grad_q, grad_k, loss_rows), ("ctx", "dp"))
    own_loss = lax.dynamic_slice_in_dim(loss_rows, dp_index, 1, 0)
    return (grad_q, grad_k, own_loss)


def solution(mesh):
    placed = (
        P("dp", "ctx", "head"),
        P("dp", "ctx", "head"),
        P("dp"),
        P("dp"),
        P("head", None, None),
        P("head", None, None),
    )
    return jax.shard_map(
        per_device,
        mesh=mesh,
        in_specs=placed,
        out_specs=(P("head", None, None), P("head", None, None), P("dp", "head")),
        check_vma=False,
    )
```

profile of v0, /device:TPU:1, one launch (start us, length us, event | category | flops | bytes accessed | tf_op | source)
XLA Modules:
  0.0 1564.9 jit_solution(13894192004086449965)
XLA Ops:
  7.2 0.0 all-gather.2.cloned.1.call-start
  7.2 2.3 copy.34
  9.6 0.0 all-gather.2.cloned.1.call-update
  9.6 0.0 all-reduce.3.cloned.1.call-start
  9.6 2.2 copy.36
  11.8 1.7 reshape.145
  14.8 0.2 bitcast_reduce_fusion.1
  15.0 0.6 compare_and_fusion
  15.6 0.6 copy-done.5
  16.2 1.0 fusion.20
  17.2 108.2 %all-gather.2.cloned.1.call-done = bf16[1,16384,512]{1,2,0:T(8,128)(2,1)} async-done(((bf16[1,1024,512]{1,2,0:T(8,128)(2,1)}), bf16[1,16384,512]{1,2,0:T(8,128)(2,1)}) %all-gather.2.cloned.1.call-update) | async-done | bytes 16777232 | tf_op jit(solution)/shard_map/all_gather | solution.py:77
  125.4 21.2 %copy.35 = bf16[4,16384,128]{2,1,0:T(8,128)(2,1)} copy(bf16[4,16384,128]{1,2,0:T(8,128)(2,1)} %bitcast.72) | data formatting | bytes 33554432 | tf_op jit(solution)/shard_map/transpose | solution.py:79
  146.6 10.1 bitcast_reduce_fusion
  156.7 0.8 copy-done.2
  157.5 10.5 convert_reduce_fusion
  167.9 820.0 %while.11 = (s32[]{:T(128)}, f32[4,2,256]{2,1,0:T(2,128)S(1)}, s32[]{:T(128)}, s32[]{:T(128)}, bf16[4,16384,128]{2,1,0:T(8,128)(2,1)}, /*index=5*/bf16[4,128,5,128]{1,3,2,0:T(8,128)(2,1)}) while((s32[]{:T(128)}, f32[4,2,256]{2,1,0:T(2,128)S(1)}, s32[]{:T(128)}, s32[]{:T(128)}, bf16[4,16384,128]{2,1,0:T(8,128)(2,1)}, ...), condition=%wide.region_11.12_spmd.clone, body=%wide.region_6.0_spmd.sunk.clone | while | flops 2835364864 | bytes 390308416 | solution.py:86
  167.9 0.7 iota_compare_fusion.4
  168.7 8.5 fusion.52
  177.2 18.3 %fusion.53 = (f32[5,128]{1,0:T(8,128)S(1)}, f32[16384,128,5]{1,0,2:T(8,128)}) fusion(pred[128,16384]{0,1:T(8,128)(4,1)S(1)} %fusion.52, bf16[4,128,5,128]{1,3,2,0:T(8,128)(2,1)} %get-tuple-element.156, s32[]{:T(128)S(6)} %copy.53, bf16[4,16384,128]{2,1,0:T(8,128)(2,1)} %get-tuple-element.155), kind=kOutput, calls=%fused_computation.2.clone.1.clone | convolution fusion | flops 2715811328 | bytes 48401920 | tf_op jit(solution)/shard_map/while/body/eval_jaxpr/qhd,kd->hqk/dot_general | solution.py:17
  195.4 18.2 %fusion.54 = f32[5,128]{1,0:T(8,128)S(1)} fusion(f32[16384,128,5]{1,0,2:T(8,128)} %get-tuple-element.128, f32[5,128]{1,0:T(8,128)S(1)} %get-tuple-element.129, pred[128,16384]{0,1:T(8,128)(4,1)S(1)} %fusion.52), kind=kLoop, calls=%fused_computation.4.clone.1.clone | loop fusion | flops 52428160 | bytes 44045312 | tf_op jit(solution)/shard_map/while/body/eval_jaxpr/reduce_sum | solution.py:26
  213.6 31.1 %fusion.55 = f32[5,128,16384]{1,2,0:T(8,128)} fusion(f32[16384,128,5]{1,0,2:T(8,128)} %get-tuple-element.128, f32[5,128]{1,0:T(8,128)S(1)} %fusion.54, f32[5,128]{1,0:T(8,128)S(1)} %get-tuple-element.129, pred[128,16384]{0,1:T(8,128)(4,1)S(1)} %fusion.52), kind=kLoop, calls=%fused_computation.3.clone.1.clone | loop fusion | flops 52428800 | bytes 85988352 | tf_op jit(solution)/shard_map/while/body/eval_jaxpr/div | solution.py:26
  244.7 42.8 %copy.49 = f32[5,128,16384]{2,1,0:T(8,128)} copy(f32[5,128,16384]{1,2,0:T(8,128)} %fusion.55) | data formatting | bytes 83886080 | tf_op jit(solution)/shard_map/while/body/eval_jaxpr/div | solution.py:26
  287.6 59.6 %reshape.151 = f32[5,2,64,256,64]{4,3,2,1,0:T(8,128)} reshape(f32[5,128,16384]{2,1,0:T(8,128)} %copy.49) | data formatting | bytes 83886080 | tf_op jit(solution)/shard_map/while/body/eval_jaxpr/reshape | solution.py:27
  347.1 25.8 %reduce_max.47 = f32[5,2,256]{2,1,0:T(2,128)S(1)} reduce(f32[5,2,64,256,64]{4,3,2,1,0:T(8,128)} %reshape.151, f32[]{:T(128)} %constant.23.clone.2..sunk.1), dimensions={2,4}, to_apply=%region_9.9 | reduce | flops 10483200 | bytes 41953284 | tf_op jit(solution)/shard_map/while/body/eval_jaxpr/reduce_max | solution.py:27
  373.0 0.7 iota_compare_fusion.4
  373.6 8.5 fusion.52
  382.1 18.3 %fusion.53 = (f32[5,128]{1,0:T(8,128)S(1)}, f32[16384,128,5]{1,0,2:T(8,128)}) fusion(pred[128,16384]{0,1:T(8,128)(4,1)S(1)} %fusion.52, bf16[4,128,5,128]{1,3,2,0:T(8,128)(2,1)} %get-tuple-element.156, s32[]{:T(128)S(6)} %copy.53, bf16[4,16384,128]{2,1,0:T(8,128)(2,1)} %get-tuple-element.155), kind=kOutput, calls=%fused_computation.2.clone.1.clone | convolution fusion | flops 2715811328 | bytes 48401920 | tf_op jit(solution)/shard_map/while/body/eval_jaxpr/qhd,kd->hqk/dot_general | solution.py:17
  400.4 18.2 %fusion.54 = f32[5,128]{1,0:T(8,128)S(1)} fusion(f32[16384,128,5]{1,0,2:T(8,128)} %get-tuple-element.128, f32[5,128]{1,0:T(8,128)S(1)} %get-tuple-element.129, pred[128,16384]{0,1:T(8,128)(4,1)S(1)} %fusion.52), kind=kLoop, calls=%fused_computation.4.clone.1.clone | loop fusion | flops 52428160 | bytes 44045312 | tf_op jit(solution)/shard_map/while/body/eval_jaxpr/reduce_sum | solution.py:26
  418.6 31.1 %fusion.55 = f32[5,128,16384]{1,2,0:T(8,128)} fusion(f32[16384,128,5]{1,0,2:T(8,128)} %get-tuple-element.128, f32[5,128]{1,0:T(8,128)S(1)} %fusion.54, f32[5,128]{1,0:T(8,128)S(1)} %get-tuple-element.129, pred[128,16384]{0,1:T(8,128)(4,1)S(1)} %fusion.52), kind=kLoop, calls=%fused_computation.3.clone.1.clone | loop fusion | flops 52428800 | bytes 85988352 | tf_op jit(solution)/shard_map/while/body/eval_jaxpr/div | solution.py:26
  449.6 42.8 %copy.49 = f32[5,128,16384]{2,1,0:T(8,128)} copy(f32[5,128,16384]{1,2,0:T(8,128)} %fusion.55) | data formatting | bytes 83886080 | tf_op jit(solution)/shard_map/while/body/eval_jaxpr/div | solution.py:26
  492.5 59.6 %reshape.151 = f32[5,2,64,256,64]{4,3,2,1,0:T(8,128)} reshape(f32[5,128,16384]{2,1,0:T(8,128)} %copy.49) | data formatting | bytes 83886080 | tf_op jit(solution)/shard_map/while/body/eval_jaxpr/reshape | solution.py:27
  552.1 25.8 %reduce_max.47 = f32[5,2,256]{2,1,0:T(2,128)S(1)} reduce(f32[5,2,64,256,64]{4,3,2,1,0:T(8,128)} %reshape.151, f32[]{:T(128)} %constant.23.clone.2..sunk.1), dimensions={2,4}, to_apply=%region_9.9 | reduce | flops 10483200 | bytes 41953284 | tf_op jit(solution)/shard_map/while/body/eval_jaxpr/reduce_max | solution.py:27
  577.9 0.7 iota_compare_fusion.4
  578.6 8.5 fusion.52
  587.0 18.3 %fusion.53 = (f32[5,128]{1,0:T(8,128)S(1)}, f32[16384,128,5]{1,0,2:T(8,128)}) fusion(pred[128,16384]{0,1:T(8,128)(4,1)S(1)} %fusion.52, bf16[4,128,5,128]{1,3,2,0:T(8,128)(2,1)} %get-tuple-element.156, s32[]{:T(128)S(6)} %copy.53, bf16[4,16384,128]{2,1,0:T(8,128)(2,1)} %get-tuple-element.155), kind=kOutput, calls=%fused_computation.2.clone.1.clone | convolution fusion | flops 2715811328 | bytes 48401920 | tf_op jit(solution)/shard_map/while/body/eval_jaxpr/qhd,kd->hqk/dot_general | solution.py:17
  605.3 18.2 %fusion.54 = f32[5,128]{1,0:T(8,128)S(1)} fusion(f32[16384,128,5]{1,0,2:T(8,128)} %get-tuple-element.128, f32[5,128]{1,0:T(8,128)S(1)} %get-tuple-element.129, pred[128,16384]{0,1:T(8,128)(4,1)S(1)} %fusion.52), kind=kLoop, calls=%fused_computation.4.clone.1.clone | loop fusion | flops 52428160 | bytes 44045312 | tf_op jit(solution)/shard_map/while/body/eval_jaxpr/reduce_sum | solution.py:26
  623.5 31.1 %fusion.55 = f32[5,128,16384]{1,2,0:T(8,128)} fusion(f32[16384,128,5]{1,0,2:T(8,128)} %get-tuple-element.128, f32[5,128]{1,0:T(8,128)S(1)} %fusion.54, f32[5,128]{1,0:T(8,128)S(1)} %get-tuple-element.129, pred[128,16384]{0,1:T(8,128)(4,1)S(1)} %fusion.52), kind=kLoop, calls=%fused_computation.3.clone.1.clone | loop fusion | flops 52428800 | bytes 85988352 | tf_op jit(solution)/shard_map/while/body/eval_jaxpr/div | solution.py:26
  654.6 42.8 %copy.49 = f32[5,128,16384]{2,1,0:T(8,128)} copy(f32[5,128,16384]{1,2,0:T(8,128)} %fusion.55) | data formatting | bytes 83886080 | tf_op jit(solution)/shard_map/while/body/eval_jaxpr/div | solution.py:26
  697.4 59.6 %reshape.151 = f32[5,2,64,256,64]{4,3,2,1,0:T(8,128)} reshape(f32[5,128,16384]{2,1,0:T(8,128)} %copy.49) | data formatting | bytes 83886080 | tf_op jit(solution)/shard_map/while/body/eval_jaxpr/reshape | solution.py:27
  757.0 25.8 %reduce_max.47 = f32[5,2,256]{2,1,0:T(2,128)S(1)} reduce(f32[5,2,64,256,64]{4,3,2,1,0:T(8,128)} %reshape.151, f32[]{:T(128)} %constant.23.clone.2..sunk.1), dimensions={2,4}, to_apply=%region_9.9 | reduce | flops 10483200 | bytes 41953284 | tf_op jit(solution)/shard_map/while/body/eval_jaxpr/reduce_max | solution.py:27
  782.8 0.7 iota_compare_fusion.4
  783.5 8.5 fusion.52
  792.0 18.3 %fusion.53 = (f32[5,128]{1,0:T(8,128)S(1)}, f32[16384,128,5]{1,0,2:T(8,128)}) fusion(pred[128,16384]{0,1:T(8,128)(4,1)S(1)} %fusion.52, bf16[4,128,5,128]{1,3,2,0:T(8,128)(2,1)} %get-tuple-element.156, s32[]{:T(128)S(6)} %copy.53, bf16[4,16384,128]{2,1,0:T(8,128)(2,1)} %get-tuple-element.155), kind=kOutput, calls=%fused_computation.2.clone.1.clone | convolution fusion | flops 2715811328 | bytes 48401920 | tf_op jit(solution)/shard_map/while/body/eval_jaxpr/qhd,kd->hqk/dot_general | solution.py:17
  810.2 18.2 %fusion.54 = f32[5,128]{1,0:T(8,128)S(1)} fusion(f32[16384,128,5]{1,0,2:T(8,128)} %get-tuple-element.128, f32[5,128]{1,0:T(8,128)S(1)} %get-tuple-element.129, pred[128,16384]{0,1:T(8,128)(4,1)S(1)} %fusion.52), kind=kLoop, calls=%fused_computation.4.clone.1.clone | loop fusion | flops 52428160 | bytes 44045312 | tf_op jit(solution)/shard_map/while/body/eval_jaxpr/reduce_sum | solution.py:26
  828.4 31.1 %fusion.55 = f32[5,128,16384]{1,2,0:T(8,128)} fusion(f32[16384,128,5]{1,0,2:T(8,128)} %get-tuple-element.128, f32[5,128]{1,0:T(8,128)S(1)} %fusion.54, f32[5,128]{1,0:T(8,128)S(1)} %get-tuple-element.129, pred[128,16384]{0,1:T(8,128)(4,1)S(1)} %fusion.52), kind=kLoop, calls=%fused_computation.3.clone.1.clone | loop fusion | flops 52428800 | bytes 85988352 | tf_op jit(solution)/shard_map/while/body/eval_jaxpr/div | solution.py:26
  859.5 42.8 %copy.49 = f32[5,128,16384]{2,1,0:T(8,128)} copy(f32[5,128,16384]{1,2,0:T(8,128)} %fusion.55) | data formatting | bytes 83886080 | tf_op jit(solution)/shard_map/while/body/eval_jaxpr/div | solution.py:26
  902.4 59.6 %reshape.151 = f32[5,2,64,256,64]{4,3,2,1,0:T(8,128)} reshape(f32[5,128,16384]{2,1,0:T(8,128)} %copy.49) | data formatting | bytes 83886080 | tf_op jit(solution)/shard_map/while/body/eval_jaxpr/reshape | solution.py:27
  961.9 25.8 %reduce_max.47 = f32[5,2,256]{2,1,0:T(2,128)S(1)} reduce(f32[5,2,64,256,64]{4,3,2,1,0:T(8,128)} %reshape.151, f32[]{:T(128)} %constant.23.clone.2..sunk.1), dimensions={2,4}, to_apply=%region_9.9 | reduce | flops 10483200 | bytes 41953284 | tf_op jit(solution)/shard_map/while/body/eval_jaxpr/reduce_max | solution.py:27
  988.0 2.1 fusion.19
  990.1 0.5 fusion.17
  990.7 0.2 select_reduce_fusion
  990.8 0.1 reduce_sum.66
  990.9 0.1 fusion.16
  991.0 0.4 convolution_multiply_fusion.2
  991.4 1.0 convolution_multiply_fusion
  992.5 4.6 fusion.18
  997.0 4.0 fusion.22
  1001.1 0.2 fusion.27
  1001.3 0.1 broadcast_multiply_fusion.2
  1001.4 138.7 %psum.23 = f32[4,4]{1,0:T(4,128)S(1)} all-reduce(f32[4,4]{1,0:T(4,128)S(1)} %broadcast_multiply_fusion.2), channel_id=1, replica_groups=mesh['ctx'=16,'head'=2,'dp'=4] {'ctx','dp'}, use_global_device_ids=true, to_apply=%region_16.17 | all-reduce | flops 16 | bytes 128 | tf_op jit(solution)/shard_map/psum | solution.py:111
  1140.0 0.5 constant_dynamic-slice_fusion
  1140.6 412.9 %all-reduce.3.cloned.1.call-done = (f32[4,640,128]{2,1,0:T(8,128)}, f32[4,384,128]{2,1,0:T(8,128)}) async-done(((f32[4,640,128]{2,1,0:T(8,128)}, f32[4,384,128]{2,1,0:T(8,128)}), (f32[4,640,128]{2,1,0:T(8,128)}, f32[4,384,128]{2,1,0:T(8,128)})) %all-reduce.3.cloned.1.call-update) | async-done | bytes 2097168 | tf_op jit(solution)/shard_map/psum | solution.py:111
  1553.5 2.5 copy.61
  1556.0 2.1 copy.62
  (36 shorter events, 0.3 us)
Async XLA Ops:
  7.2 9.0 copy-start
  7.2 118.2 %all-gather.2.cloned.1.call-start = ((), (), s32[]{:S(2)}) async-start(), calls=%async_computation | async-start | bytes 17825792 | tf_op jit(solution)/shard_map/all_gather | solution.py:77
  9.6 1543.9 %all-reduce.3.cloned.1.call-start = ((), (), s32[]{:S(2)}) async-start(), calls=%async_computation.1 | async-start | bytes 4194304 | tf_op jit(solution)/shard_map/psum | solution.py:111
  15.6 0.6 copy-start.5
  146.6 10.9 copy-start.2
  167.9 820.0 %copy-start.3 = (f32[4,256,128]{2,1,0:T(8,128)S(1)}, f32[4,256,128]{2,1,0:T(8,128)}, u32[]{:S(2)}) copy-start(f32[4,256,128]{2,1,0:T(8,128)} %get-tuple-element.61) | copy-start | bytes 1572868
  167.9 820.1 %copy-start.4 = (bf16[4,256,128]{2,1,0:T(8,128)(2,1)S(1)}, bf16[4,256,128]{2,1,0:T(8,128)(2,1)}, u32[]{:S(2)}) copy-start(bf16[4,256,128]{2,1,0:T(8,128)(2,1)} %bitcast_reduce_fusion) | copy-start | bytes 786436
  167.9 822.2 %copy-start.6 = (f32[4,2,128]{2,1,0:T(2,128)S(1)}, f32[4,2,128]{2,1,0:T(2,128)}, u32[]{:S(2)}) copy-start(f32[4,2,128]{2,1,0:T(2,128)} %fusion.20) | copy-start | bytes 12292
  167.9 822.2 %copy-start.7 = (pred[2,256]{1,0:T(4,128)(4,1)S(1)}, pred[2,256]{1,0:T(4,128)(4,1)}, u32[]{:S(2)}) copy-start(pred[2,256]{1,0:T(4,128)(4,1)} %compare_and_fusion) | copy-start | bytes 1540
  987.9 570.1 %copy-start.1 = (bf16[4,640,128]{2,1,0:T(8,128)(2,1)S(1)}, bf16[4,640,128]{2,1,0:T(8,128)(2,1)}, u32[]{:S(2)}) copy-start(bf16[4,640,128]{2,1,0:T(8,128)(2,1)} %param.12) | copy-start | bytes 1966084
Sparse Core Ops, SparseCore 0:
  10.7 114.6 all-gather.1
  1001.2 552.2 all-reduce.2
where the time goes:
time: 1580 us; the launch traced here: 1560 us
  waiting for transfers between devices  521 us (33%)
  local copies, waits for them, and re-layouts  443 us (28%)
  other arithmetic  359 us (23%)
  blocking collectives  139 us (9%)
  matrix products  86.7 us (5%)
    psum x1, waiting for transfers between devices, per_device(): lax.psum((grad_q, grad_k, loss_rows), ('ctx', 'dp'))  413 us
    reshape x4, local copies, waits for them, and re-layouts, teacher_rows(): probs.reshape(GROUP, row_count // BLK, BLK, ctx_len // BLK, BLK)  238 us
    div x4, local copies, waits for them, and re-layouts, teacher_rows(): probs = weights / jnp.sum(weights, axis=2, keepdims=True)  171 us
    psum x1, blocking collectives, per_device(): lax.psum((grad_q, grad_k, loss_rows), ('ctx', 'dp'))  139 us
    div x4, other arithmetic, teacher_rows(): probs = weights / jnp.sum(weights, axis=2, keepdims=True)  124 us
    all_gather x1, waiting for transfers between devices, per_device(): whole_keys = lax.all_gather(keys, 'ctx', axis=1, tiled=True)[0]  108 us
    reduce_max x4, other arithmetic, teacher_rows(): probs.reshape(GROUP, row_count // BLK, BLK, ctx_len // BLK, BLK)  103 us
    dot_general x4, matrix products, teacher_rows(): jnp.einsum('qhd,kd->hqk', rows, key_group, preferred_element_type=jnp.flo...  73.1 us
  transfers between devices with their start and end apart: 2, of which 2 were waited for; matrix products, arithmetic and copies ran while one was open for 0% of the time, Pallas kernels for 0%

commit v1 on v0

v1 whole, which is shorter than its diff:
```python
import functools
import math

import jax
import jax.numpy as jnp
from jax import lax
from jax.experimental import pallas as pl
from jax.experimental.pallas import tpu as pltpu
from jax.sharding import Mesh, PartitionSpec as P

BLK = 64
GROUP = 5
HD = 128
QB = 32
NEG = -1e30
FLOOR = -1e20
KT = 512
KB = KT // BLK
SCALE = HD ** -0.5
SCALE2 = SCALE * math.log2(math.e)
VMEM = 56 * 2 ** 20
F32 = jnp.float32
BF16 = jnp.bfloat16
NT = (((1,), (1,)), ((), ()))
TN = (((0,), (0,)), ((), ()))
NN = (((1,), (0,)), ((), ()))


def split2(x):
    hi = x.astype(BF16)
    return hi, (x - hi.astype(F32)).astype(BF16)


def mm(a, b, dims):
    return lax.dot_general(a, b, dims, preferred_element_type=F32)


def dot2(a, b, dims):
    hi, lo = split2(a)
    return mm(hi, b, dims) + mm(lo, b, dims)


def dot3(a, b, dims):
    ah, al = split2(a)
    bh, bl = split2(b)
    return mm(ah, bh, dims) + (mm(ah, bl, dims) + mm(al, bh, dims))


def block_update(s, m, l, floor):
    rt = s.shape[1]
    tops = []
    for j in range(KB):
        sj = s[j * BLK:(j + 1) * BLK]
        top = sj.reshape(8, 8, rt).max(axis=0).max(axis=0, keepdims=True)
        tops.append(top)
        if floor:
            top = jnp.maximum(top, FLOOR)
        if m is None:
            m = top
            l = jnp.exp2(sj - m).reshape(8, 8, rt).sum(axis=0)
        else:
            new = jnp.maximum(m, top)
            l = l * jnp.exp2(m - new) + jnp.exp2(sj - new).reshape(8, 8, rt).sum(axis=0)
            m = new
    return jnp.concatenate(tops, axis=0), m, l


def scores_kernel(pos_ref, *refs, q_rows, k_rows, shards):
    nq, nk = len(q_rows), len(k_rows)
    q_refs, k_refs = refs[:nq], refs[nq:nq + nk]
    bm_ref, ml_ref, qs, m_s, l_s = refs[nq + nk:]
    rt = sum(q_rows)
    tiles = [(p, o) for p in range(nk) for o in range(0, k_rows[p], KT)]
    q_at, t_at = shards, shards + nq
    for h in range(GROUP):
        for p in range(nq):
            x = q_refs[p][:, h * HD:(h + 1) * HD].astype(F32) * SCALE2
            hi, lo = split2(x)
            at = pl.multiple_of(pos_ref[q_at + p], BLK)
            qs[h, pl.ds(at, q_rows[p]), :] = jnp.concatenate([hi, lo], axis=1)
    q_pos = [pos_ref[i] for i in range(shards)]
    low = functools.reduce(jnp.minimum, q_pos)
    high = functools.reduce(jnp.maximum, q_pos) + 1
    kp = [pos_ref[t_at + 2 * t] for t in range(len(tiles))]
    out = [pl.multiple_of(pos_ref[t_at + 2 * t + 1], KB) for t in range(len(tiles))]
    full = functools.reduce(jnp.maximum, kp) + KB - 1 < low

    def scores(t, h):
        p, o = tiles[t]
        k = k_refs[p][o:o + KT, :]
        return mm(jnp.concatenate([k, k], axis=1), qs[h], NT)

    def head(h, _):
        @pl.when(full)
        def _():
            m = l = None
            for t in range(len(tiles)):
                top, m, l = block_update(scores(t, h), m, l, False)
                bm_ref[0, h, pl.ds(out[t], KB), :] = top
            ml_ref[0, h, 0:1, :] = m
            ml_ref[0, h, 1:2, :] = l.sum(axis=0, keepdims=True)

        @pl.when(jnp.logical_not(full))
        def _():
            m_s[...] = jnp.full(m_s.shape, FLOOR, F32)
            l_s[...] = jnp.zeros(l_s.shape, F32)
            lane = lax.broadcasted_iota(jnp.int32, (1, rt), 1)
            q_row = lane % 128
            for i in range(shards):
                q_row = q_row + jnp.where(lane // 128 == i, q_pos[i] * BLK, 0)
            for t in range(len(tiles)):
                none = kp[t] > high

                @pl.when(jnp.logical_not(none))
                def _():
                    k_row = kp[t] * BLK + lax.broadcasted_iota(jnp.int32, (KT, rt), 0)
                    s = jnp.where(k_row <= q_row, scores(t, h), NEG)
                    top, m, l = block_update(s, m_s[...], l_s[...], True)
                    bm_ref[0, h, pl.ds(out[t], KB), :] = top
                    m_s[...] = m
                    l_s[...] = l

                @pl.when(none)
                def _():
                    bm_ref[0, h, pl.ds(out[t], KB), :] = jnp.full((KB, rt), NEG, F32)

            ml_ref[0, h, 0:1, :] = m_s[...]
            ml_ref[0, h, 1:2, :] = l_s[...].sum(axis=0, keepdims=True)

        return 0

    lax.fori_loop(0, GROUP, head, 0)


def block_scores(pos, q_parts, k_parts, shards):
    q_rows = [q.shape[0] for q in q_parts]
    k_rows = [k.shape[0] for k in k_parts]
    rt, kn = sum(q_rows), sum(k_rows)
    groups = k_parts[0].shape[1] // HD
    return pl.pallas_call(
        functools.partial(scores_kernel, q_rows=q_rows, k_rows=k_rows, shards=shards),
        grid_spec=pltpu.PrefetchScalarGridSpec(
            num_scalar_prefetch=1,
            grid=(groups,),
            in_specs=[pl.BlockSpec((r, GROUP * HD), lambda g, p: (0, g)) for r in q_rows]
            + [pl.BlockSpec((r, HD), lambda g, p: (0, g)) for r in k_rows],
            out_specs=[
                pl.BlockSpec((1, GROUP, kn // BLK, rt), lambda g, p: (g, 0, 0, 0)),
                pl.BlockSpec((1, GROUP, 2, rt), lambda g, p: (g, 0, 0, 0)),
            ],
            scratch_shapes=[
                pltpu.VMEM((GROUP, rt, 2 * HD), BF16),
                pltpu.VMEM((1, rt), F32),
                pltpu.VMEM((8, rt), F32),
            ],
        ),
        out_shape=[
            jax.ShapeDtypeStruct((groups, GROUP, kn // BLK, rt), F32),
            jax.ShapeDtypeStruct((groups, GROUP, 2, rt), F32),
        ],
        compiler_params=pltpu.CompilerParams(vmem_limit_bytes=VMEM),
        cost_estimate=pl.CostEstimate(
            flops=4 * groups * GROUP * rt * kn * HD,
            bytes_accessed=4 * groups * GROUP * rt * kn // BLK,
            transcendentals=groups * GROUP * rt * kn,
        ),
        name="block_scores",
    )(pos, *q_parts, *k_parts)


def teacher_kernel(bm_ref, *refs):
    ml_refs, out_ref = refs[:-1], refs[-1]
    nb, rt = bm_ref.shape[2], bm_ref.shape[3]
    row = lax.broadcasted_iota(jnp.int32, (rt // BLK, rt), 0)
    lane = lax.broadcasted_iota(jnp.int32, (rt // BLK, rt), 1)
    pick = (lane == row * BLK).astype(BF16)
    halves = []
    for gg in range(2):
        total = None
        for h in range(GROUP):
            ms = [r[gg, h, 0:1, :] for r in ml_refs]
            m = functools.reduce(jnp.maximum, ms)
            l = sum(r[gg, h, 1:2, :] * jnp.exp2(mi - m) for r, mi in zip(ml_refs, ms))
            e = jnp.exp2(bm_ref[gg, h] - m) * (1.0 / l)
            cols = []
            for c in range(0, rt, 128):
                x = e[:, c:c + 128]
                for sh in (1, 2, 4, 8, 16, 32):
                    x = jnp.maximum(x, pltpu.roll(x, 128 - sh, 1))
                cols.append(x)
            x = jnp.concatenate(cols, axis=1)
            total = x if total is None else total + x
        total = total * (1.0 / GROUP)
        hi, lo = split2(total)
        lo2 = (total - hi.astype(F32) - lo.astype(F32)).astype(BF16)
        halves.append(mm(pick, hi, NT) + (mm(pick, lo, NT) + mm(pick, lo2, NT)))
    out_ref[0] = jnp.concatenate(halves, axis=1)


def teacher_blocks(bm, mls):
    groups, _, nb, rt = bm.shape
    return pl.pallas_call(
        teacher_kernel,
        grid=(groups // 2,),
        in_specs=[pl.BlockSpec((2, GROUP, nb, rt), lambda g: (g, 0, 0, 0))]
        + [pl.BlockSpec((2, GROUP, 2, rt), lambda g: (g, 0, 0, 0))] * len(mls),
        out_specs=pl.BlockSpec((1, rt // BLK, 2 * nb), lambda g: (g, 0, 0)),
        out_shape=jax.ShapeDtypeStruct((groups // 2, rt // BLK, 2 * nb), F32),
        compiler_params=pltpu.CompilerParams(vmem_limit_bytes=VMEM),
        name="teacher",
    )(bm, *mls)


def grads_kernel(pos_ref, pk0_ref, pk1_ref, pq_ref, t_ref, wq_ref, wk_ref, gq_ref, gk_ref, loss_ref):
    gp = pl.program_id(0)
    own_y, own_c = pos_ref[4], pos_ref[5]
    for gg in range(2):
        g = gp * 2 + gg
        d_qs, d_ks, pks = [], [], [[], [], []]
        loss_own = jnp.zeros((1, 1), F32)
        for si in range(4):
            crel, y = si // 2, si % 2
            c = jnp.where(own_c == crel, 0, 1)
            start = pos_ref[y * 2 + c]
            pk_ref = (pk0_ref, pk1_ref)[crel]
            parts = []
            for p in range(3):
                at = pl.multiple_of((g * 3 + p) * 16, 16)
                x = pk_ref[:, :, y, pl.ds(at, 16), :].reshape(256, 128)
                parts.append(x)
                pks[p].append(x)
            proj_k = sum(dot2(parts[p], wk_ref[gg, p * 128:(p + 1) * 128, :], NN) for p in range(3))
            pq = pq_ref[gg, si * QB:(si + 1) * QB, :]
            proj_q = dot2(pq, wq_ref[gg], NN)
            logits = dot3(proj_q, proj_k, NT) * SCALE
            row = lax.broadcasted_iota(jnp.int32, (QB, 256), 0)
            col = lax.broadcasted_iota(jnp.int32, (QB, 256), 1)
            a = (row % 8) // 2 * 8 + row // 8 * 2 + row % 2
            live = col <= start + a
            masked = jnp.where(live, logits, NEG)
            top = masked.max(axis=1, keepdims=True)
            ex = jnp.where(live, jnp.exp(masked - top), 0.0)
            total = ex.sum(axis=1, keepdims=True)
            gate = ex / total
            log_gate = masked - top - jnp.log(total)
            teacher = jnp.concatenate(
                [
                    jnp.concatenate(
                        [t_ref[z, x, y, c, 0, :, gg * 64:(gg + 1) * 64] for z in range(4)], axis=1
                    )
                    for x in range(4)
                ],
                axis=0,
            )
            target = teacher / teacher.sum(axis=1, keepdims=True)
            some = target > 0.0
            term = jnp.where(some, target * jnp.log(jnp.where(some, target, 1.0)), 0.0)
            term = term - jnp.where(live, target * log_gate, 0.0)
            if crel == 0:
                val = term.sum(axis=1, keepdims=True).sum(axis=0, keepdims=True) * (1.0 / QB)
                loss_own = loss_own + jnp.where(own_y == y, val, 0.0)
            slope = (gate - target) * (1.0 / QB)
            d_qs.append(dot3(slope, proj_k, NN) * SCALE)
            d_ks.append(dot3(slope, proj_q, TN) * SCALE)
        gq_ref[gg] = dot3(pq_ref[gg], jnp.concatenate(d_qs, axis=0), TN)
        d_k = jnp.concatenate(d_ks, axis=0)
        for p in range(3):
            gk_ref[gg, p * 128:(p + 1) * 128, :] = dot3(jnp.concatenate(pks[p], axis=0), d_k, TN)
        loss_ref[0, gg:gg + 1, :] = jnp.broadcast_to(loss_own, (1, 128))


def gate_gradients(pos, pk0, pk1, pq, teachers, wq, wk):
    groups = wq.shape[0]
    whole = lambda x: pl.BlockSpec(x.shape, lambda g, p: (0,) * x.ndim)
    pair = lambda x: pl.BlockSpec((2,) + x.shape[1:], lambda g, p: (g, 0, 0))
    return pl.pallas_call(
        grads_kernel,
        grid_spec=pltpu.PrefetchScalarGridSpec(
            num_scalar_prefetch=1,
            grid=(groups // 2,),
            in_specs=[
                whole(pk0),
                whole(pk1),
                pair(pq),
                pl.BlockSpec((4, 4, 2, 2, 1, 8, 128), lambda g, p: (0, 0, 0, 0, g, 0, 0)),
                pair(wq),
                pair(wk),
            ],
            out_specs=[
                pl.BlockSpec((2,) + wq.shape[1:], lambda g, p: (g, 0, 0)),
                pl.BlockSpec((2,) + wk.shape[1:], lambda g, p: (g, 0, 0)),
                pl.BlockSpec((1, 2, 128), lambda g, p: (g, 0, 0)),
            ],
        ),
        out_shape=[
            jax.ShapeDtypeStruct(wq.shape, F32),
            jax.ShapeDtypeStruct(wk.shape, F32),
            jax.ShapeDtypeStruct((groups // 2, 2, 128), F32),
        ],
        compiler_params=pltpu.CompilerParams(vmem_limit_bytes=VMEM),
        name="gate_gradients",
    )(pos, pk0, pk1, pq, teachers, wq, wk)


def shift(x, axis, by):
    return lax.ppermute(x, axis, [(i, (i + by) % 4) for i in range(4)])


def ring_parts(x, axis):
    half = x.shape[0] // 2
    before, after = shift(x, axis, 1), shift(x, axis, -1)
    return [x, before, after, shift(before[:half], axis, 1), shift(after[half:], axis, -1)]


def per_device(queries, keys, start_block, lengths, gate_query, gate_key):
    del lengths
    z, x = lax.axis_index("z"), lax.axis_index("x")
    y, c = lax.axis_index("y"), lax.axis_index("c")
    q, k = queries[0], keys[0]
    start = start_block[0]
    starts = lax.all_gather(start_block, ("y", "c"), tiled=True)
    q_mean = q.astype(F32).reshape(2, BLK, 4, GROUP, HD).mean(axis=1)
    kf = k.astype(F32).reshape(16, BLK, 4, HD)
    k_pool = jnp.stack([kf.max(axis=1), kf.min(axis=1), kf.mean(axis=1)], axis=2)
    pack = jnp.concatenate(
        [k_pool.transpose(1, 2, 0, 3).reshape(192, HD), q_mean.reshape(40, HD)], axis=0
    )
    pack = lax.all_gather(pack, "y")
    pack = lax.all_gather(pack, "x")
    pack = lax.all_gather(pack, "z")
    other = lax.ppermute(pack, "c", [(0, 1), (1, 0)])
    pq = jnp.stack([pack[..., 192:, :], other[..., 192:, :]])
    pq = pq.reshape(2, 4, 4, 2, 2, 4, GROUP * HD).transpose(5, 0, 3, 2, 1, 4, 6)
    pq = pq.reshape(4, 4 * QB, GROUP * HD)
    q_parts = ring_parts(q, "z")
    k_parts = ring_parts(k, "x")
    zs = [z, (z + 3) % 4, (z + 1) % 4, (z + 2) % 4]
    xs = [x, (x + 3) % 4, (x + 1) % 4, (x + 2) % 4]
    q_pos = [start + (zz * 4 + x) * 2 for zz in range(4)]
    q_at = [zs[0] * 128, zs[1] * 128, zs[2] * 128, zs[3] * 128, zs[3] * 128 + 64]
    t_at = []
    for xx in xs:
        for half in range(2):
            t_at += [(z * 4 + xx) * 16 + half * 8, xx * 16 + half * 8]
    pos = jnp.stack([jnp.asarray(v, jnp.int32) for v in q_pos + q_at + t_at])
    bm, ml = block_scores(pos, q_parts, k_parts, 4)
    mls = [ml, shift(ml, "z", 1), shift(ml, "z", -1), shift(ml, "z", 2)]
    teacher = teacher_blocks(bm, mls)
    teachers = lax.all_to_all(
        jnp.broadcast_to(teacher[None], (64,) + teacher.shape), ("z", "x", "y", "c"), 0, 0, tiled=True
    ).reshape((4, 4, 2, 2) + teacher.shape)
    pos2 = jnp.concatenate([starts, jnp.stack([y, c]).astype(jnp.int32)])
    grad_q, grad_k, loss = gate_gradients(pos2, pack, other, pq, teachers, gate_query, gate_key)
    return grad_q, grad_k, loss[:, :, 0].reshape(1, 4)


def solution(mesh):
    fine = Mesh(mesh.devices.reshape(4, 4, 2, 2, 2), ("z", "x", "h", "y", "c"))
    ctx, dp = ("z", "x"), ("y", "c")
    placed = (
        P(dp, ctx, "h"),
        P(dp, ctx, "h"),
        P(dp),
        P(dp),
        P("h", None, None),
        P("h", None, None),
    )
    return jax.shard_map(
        per_device,
        mesh=fine,
        in_specs=placed,
        out_specs=(P("h", None, None), P("h", None, None), P(dp, "h")),
        check_vma=False,
    )
```

time: 1580 us -> 279 us (0.18)
  waiting for transfers between devices: 521 us -> 70.1 us
  local copies, waits for them, and re-layouts: 443 us -> 17.6 us
  other arithmetic: 359 us -> 2.61 us
  blocking collectives: 139 us -> 24.2 us
  matrix products: 86.7 us -> 0 us
  Pallas kernels: 0 us -> 84 us
  starting transfers between devices: 0.08 us -> 65.2 us
    psum x1 -> x0, waiting for transfers between devices: 413 us -> none  [per_device(): lax.psum((grad_q, grad_k, loss_rows), ('ctx', 'dp'))]
    reshape x5 -> x1, local copies, waits for them, and re-layouts: 240 us -> 2.06 us  [per_device(): pq = pq.reshape(4, 4 * QB, GROUP * HD)]
    div x4 -> x1, local copies, waits for them, and re-layouts: 171 us -> 0.01 us  [per_device(): q_mean = q.astype(F32).reshape(2, BLK, 4, GROUP, HD).mean(axis=1)]
    psum x1 -> x0, blocking collectives: 139 us -> none  [per_device(): lax.psum((grad_q, grad_k, loss_rows), ('ctx', 'dp'))]
    div x8 -> x2, other arithmetic: 124 us -> 0.02 us  [the longest x1 0.01 us: per_device(): kf.mean(axis=1)]
    reduce_max x6 -> x2, other arithmetic: 113 us -> 0.43 us  [per_device(): kf.max(axis=1)]
    dot_general x11 -> x0, matrix products: 86.7 us -> none  [the longest x4 73.1 us: teacher_rows(): jnp.einsum('qhd,kd->hqk', rows, key_group, preferred_element_type=jnp.flo...]
    pallas_call x0 -> x3, Pallas kernels: none -> 84 us  [the longest x1 41.6 us: block_scores(): pl.pallas_call(functools.partial(scores_kernel, q_rows=q_rows, k_rows=k_r...]
  transfers between devices with their start and end apart: 2 -> 14, of which waited for: 2 -> 7; matrix products, arithmetic and copies ran while one was open for 0% -> 4% of each run, Pallas kernels for 0% -> 23%
where the time goes in v1:
time: 279 us
  Pallas kernels  84 us (30%)
  waiting for transfers between devices  70.1 us (25%)
  starting transfers between devices  65.2 us (23%)
  blocking collectives  24.2 us (9%)
  local copies, waits for them, and re-layouts  17.6 us (6%)
  between operations  15 us (5%)
    all_gather x1, waiting for transfers between devices, per_device(): pack = lax.all_gather(pack, 'z')  49.2 us
    pallas_call x1, Pallas kernels, block_scores(): pl.pallas_call(functools.partial(scores_kernel, q_rows=q_rows, k_rows=k_r...  41.6 us
    all_to_all x1, starting transfers between devices, per_device(): lax.all_to_all(jnp.broadcast_to(teacher[None], (64,) + teacher.shape), ('...  40.5 us
    ppermute x11, starting transfers between devices, shift(): return lax.ppermute(x, axis, [(i, (i + by) % 4) for i in range(4)])  24 us
    pallas_call x1, Pallas kernels, gate_gradients(): pl.pallas_call(grads_kernel, grid_spec=pltpu.PrefetchScalarGridSpec(num_s...  21.2 us
    pallas_call x1, Pallas kernels, teacher_blocks(): pl.pallas_call(teacher_kernel, grid=(groups // 2,), in_specs=[pl.BlockSpe...  21.2 us
    ppermute x11, waiting for transfers between devices, shift(): return lax.ppermute(x, axis, [(i, (i + by) % 4) for i in range(4)])  20.9 us
    all_gather x1, blocking collectives, per_device(): pack = lax.all_gather(pack, 'x')  14.2 us
  transfers between devices with their start and end apart: 14, of which 7 were waited for; matrix products, arithmetic and copies ran while one was open for 4% of the time, Pallas kernels for 23%

profile of v1, /device:TPU:1, one launch (start us, length us, event | category | flops | bytes accessed | tf_op | source)
XLA Modules:
  0.0 278.6 jit_solution(8909253325033616974)
XLA Ops:
  7.2 0.0 all-gather.5.cloned.1.call-start
  7.2 1.3 squeeze.11
  8.6 0.0 copy-start.2
  8.6 0.7 convert_reduce_fusion.1
  9.3 0.4 reduce_max.16
  9.8 0.7 reshape.51
  10.5 0.2 reduce_sum.19
  10.7 0.0 copy-start.1
  10.7 5.1 %all-gather = f32[464,128]{1,0:T(8,128)S(1)} all-gather(f32[232,128]{1,0:T(8,128)S(1)} %pad_maximum_fusion), channel_id=2, replica_groups=mesh['z'=4,'x'=4,'h'=2,'y'=2,'c'=2] {'y'}, dimensions={0}, use_global_device_ids=true | all-gather | bytes 356352 | tf_op jit(solution)/shard_map/all_gather | solution.py:328
  15.9 14.2 %all-gather.1 = f32[8,232,128]{2,1,0:T(8,128)} all-gather(f32[2,232,128]{2,1,0:T(8,128)S(1)} %bitcast.62), channel_id=3, replica_groups=mesh['z'=4,'x'=4,'h'=2,'y'=2,'c'=2] {'x'}, dimensions={0}, use_global_device_ids=true | all-gather | bytes 1187840 | tf_op jit(solution)/shard_map/all_gather | solution.py:329
  30.1 0.0 all-gather.5.cloned.1.call-update
  30.1 0.8 collective-permute-start.6
  31.0 0.7 collective-permute-start.5
  31.7 49.2 %all-gather.5.cloned.1.call-done = f32[16,2,232,128]{3,2,1,0:T(8,128)} async-done(((f32[4,2,232,128]{3,2,1,0:T(8,128)}), f32[16,2,232,128]{3,2,1,0:T(8,128)}) %all-gather.5.cloned.1.call-update) | async-done | bytes 3801104 | tf_op jit(solution)/shard_map/all_gather | solution.py:330
  80.9 0.7 collective-permute-start
  81.5 0.5 collective-permute-start.2
  82.0 1.0 collective-permute-start.1
  83.0 0.0 collective-permute-done.6.refs_7_
  83.0 1.1 slice.33
  84.1 2.5 collective-permute-start.8
  86.6 0.0 collective-permute-done.5.refs_6_
  86.6 1.1 slice.32
  87.6 0.1 collective-permute-start.7
  87.7 10.3 %collective-permute-done.2.refs_2_ = bf16[128,2560]{1,0:T(8,128)(2,1)S(1)} collective-permute-done((bf16[128,2560]{1,0:T(8,128)(2,1)S(1)}, bf16[128,2560]{1,0:T(8,128)(2,1)S(1)}, u32[]{:S(2)}, u32[]{:S(2)}) %collective-permute-start.2) | collective-permute-done | bytes 655392 | tf_op jit(solution)/shard_map/ppermute | solution.py:306
  98.0 1.8 collective-permute-start.4
  99.8 0.0 collective-permute-done.1.refs_1_
  99.8 0.1 collective-permute-start.3
  99.9 0.7 copy-done.4
  101.3 0.7 stack.133.pos_ref
  102.0 4.7 %collective-permute-done.4.refs_4_ = bf16[64,2560]{1,0:T(8,128)(2,1)S(1)} collective-permute-done((bf16[64,2560]{1,0:T(8,128)(2,1)S(1)}, bf16[64,2560]{1,0:T(8,128)(2,1)S(1)}, u32[]{:S(2)}, u32[]{:S(2)}) %collective-permute-start.4) | collective-permute-done | bytes 327712 | tf_op jit(solution)/shard_map/ppermute | solution.py:306
  106.7 2.7 collective-permute-done.3.refs_3_
  109.4 0.0 collective-permute-done.8.refs_9_
  109.4 0.0 collective-permute-done.7.refs_8_
  109.4 0.0 copy-done.3
  109.4 0.7 copy-done.9
  110.1 41.6 %block_scores.1 = (f32[4,5,64,512]{3,2,1,0:T(8,128)}, f32[4,5,2,512]{3,2,1,0:T(2,128)}) custom-call(s32[25]{0:T(128)} %stack.133.pos_ref, bf16[128,2560]{1,0:T(8,128)(2,1)} %bitcast.63, bf16[128,2560]{1,0:T(8,128)(2,1)} %copy-done.4, bf16[128,2560]{1,0:T(8,128)(2,1)} %copy-done.3, bf16[64,2560]{1,0:T(8,128)(2,1)} %copy-done.9, bf16[64,2560]{1,0:T(8,128)(2,1)} %copy-done.8, ...), custom_call_target="tpu_custom_call" | custom-call | flops 21474836480 | bytes 2621440 | tf_op jit(solution)/shard_map/block_scores/pallas_call | solution.py:140
  151.7 15.1 %collective-permute-start.11 = (f32[4,5,2,512]{3,2,1,0:T(2,128)}, f32[4,5,2,512]{3,2,1,0:T(2,128)S(1)}, u32[]{:S(2)}, u32[]{:S(2)}) collective-permute-start(f32[4,5,2,512]{3,2,1,0:T(2,128)} %get-tuple-element.9.refs_0_), channel_id=1, source_target_pairs={{0,64},{32,96},{64,0},{96,32},{1,65},{33,97},{65,1},{97,33},{2,66}... | collective-permute-start | bytes 245768 | tf_op jit(solution)/shard_map/ppermute | solution.py:306
  166.8 0.0 collective-permute-start.10
  166.8 1.5 collective-permute-start.9
  168.3 0.6 collective-permute-done.11.refs_3_
  168.8 1.5 collective-permute-done.10.refs_2_
  170.3 1.2 collective-permute-done.9.refs_1_
  171.5 0.6 copy-done.7
  172.2 21.2 %teacher.1 = f32[2,8,128]{2,1,0:T(8,128)} custom-call(f32[4,5,64,512]{3,2,1,0:T(8,128)} %get-tuple-element.8.bm_ref, f32[4,5,2,512]{3,2,1,0:T(2,128)} %get-tuple-element.9.refs_0_, f32[4,5,2,512]{3,2,1,0:T(2,128)} %copy-done.7, f32[4,5,2,512]{3,2,1,0:T(2,128)} %copy-done.6, f32[4,5,2,512]{3,2,1,0:T(2,128)} %copy-done.5), custom_call_target="tpu_custom_call" | custom-call | tf_op jit(solution)/shard_map/teacher/pallas_call | solution.py:202
  193.3 1.5 broadcast_in_dim.2
  194.9 40.5 %all-to-all-start = ((f32[64,2,8,128]{3,2,1,0:T(8,128)}), f32[64,2,8,128]{3,2,1,0:T(8,128)S(1)}, u32[]{:S(2)}, u32[]{:S(2)}) async-start(f32[64,2,8,128]{3,2,1,0:T(8,128)} %broadcast_in_dim.2), calls=%async_computation | async-start | bytes 1048576 | tf_op jit(solution)/shard_map/all_to_all | solution.py:349
  235.4 0.6 dynamic-slice
  236.0 0.8 dynamic-update-slice
  236.7 4.8 %all-reduce = s32[4]{0:T(128)S(1)} all-reduce(s32[4]{0:T(128)S(1)} %dynamic-update-slice), channel_id=1, replica_groups=mesh['z'=4,'x'=4,'h'=2,'y'=2,'c'=2] {'y','c'}, use_global_device_ids=true, to_apply=%add | all-reduce | flops 4 | bytes 32
  241.5 0.6 pad_add_fusion.pos_ref
  242.2 1.1 slice.28
  243.3 0.2 stack.105
  243.5 0.3 copy.15
  243.9 0.0 collective-permute-done.pk1_ref
  243.9 1.1 slice.29
  245.1 0.2 stack.106
  245.3 0.3 copy.16
  245.7 0.6 maximum_bitcast_fusion
  246.3 2.1 reshape.48.pq_ref
  248.4 0.0 all-to-all-done
  248.4 0.8 copy-done
  249.2 21.2 %gate_gradients.1 = (f32[4,640,128]{2,1,0:T(8,128)}, f32[4,384,128]{2,1,0:T(8,128)}, f32[2,2,128]{2,1,0:T(2,128)}) custom-call(s32[6]{0:T(128)} %pad_add_fusion.pos_ref, f32[4,4,2,232,128]{4,3,2,1,0:T(8,128)} %bitcast.56, f32[4,4,2,232,128]{4,3,2,1,0:T(8,128)} %collective-permute-done.pk1_ref, f32[4,128,640]{2,1,0:T(8,128)} %reshape.48.pq_ref, ...), custom_call_target="tpu_custom_call" | custom-call | tf_op jit(solution)/shard_map/gate_gradients/pallas_call | solution.py:276
  270.4 0.7 slice_reduce_fusion
  271.2 0.6 reshape_squeeze.3
  (25 shorter events, 0.1 us)
Async XLA Ops:
  7.2 73.7 %all-gather.5.cloned.1.call-start = ((), (), s32[]{:S(2)}) async-start(), calls=%async_computation.1 | async-start | bytes 4751360 | tf_op jit(solution)/shard_map/all_gather | solution.py:330
  8.6 1.2 copy-start.2
  10.7 19.4 %copy-start.1 = (bf16[1,1024,512]{2,1,0:T(8,128)(2,1)S(1)}, bf16[1,1024,512]{2,1,0:T(8,128)(2,1)}, u32[]{:S(2)}) copy-start(bf16[1,1024,512]{2,1,0:T(8,128)(2,1)} %param.7) | copy-start | bytes 3145732
  30.1 52.9 %collective-permute-start.6 = (bf16[1024,512]{1,0:T(8,128)(2,1)S(1)}, bf16[1024,512]{1,0:T(8,128)(2,1)}, u32[]{:S(2)}, u32[]{:S(2)}) collective-permute-start(bf16[1024,512]{1,0:T(8,128)(2,1)S(1)} %bitcast.60), channel_id=1, source_target_pairs={{0,24},{8,0},{16,8},{24,16},{1,25},{9,1},{17,9},{25,17},{2,26},{10... | collective-permute-start | bytes 3145736 | tf_op jit(solution)/shard_map/ppermute | solution.py:306
  31.0 55.6 %collective-permute-start.5 = (bf16[1024,512]{1,0:T(8,128)(2,1)S(1)}, bf16[1024,512]{1,0:T(8,128)(2,1)}, u32[]{:S(2)}, u32[]{:S(2)}) collective-permute-start(bf16[1024,512]{1,0:T(8,128)(2,1)S(1)} %bitcast.61), channel_id=1, source_target_pairs={{0,8},{8,16},{16,24},{24,0},{1,9},{9,17},{17,25},{25,1},{2,10},{10... | collective-permute-start | bytes 3145736 | tf_op jit(solution)/shard_map/ppermute | solution.py:306
  80.9 163.0 %collective-permute-start = (f32[4,4,2,232,128]{4,3,2,1,0:T(8,128)}, f32[4,4,2,232,128]{4,3,2,1,0:T(8,128)}, u32[]{:S(2)}, u32[]{:S(2)}) collective-permute-start(f32[4,4,2,232,128]{4,3,2,1,0:T(8,128)} %bitcast.54), channel_id=1, source_target_pairs={{0,1},{1,0},{2,3},{3,2},{4,5},{5,4},{6,7},{7,6},{8,9},{9,8},{10,11... | collective-permute-start | bytes 11403272 | tf_op jit(solution)/shard_map/ppermute | solution.py:331
  81.5 16.5 %collective-permute-start.2 = (bf16[128,2560]{1,0:T(8,128)(2,1)S(1)}, bf16[128,2560]{1,0:T(8,128)(2,1)S(1)}, u32[]{:S(2)}, u32[]{:S(2)}) collective-permute-start(bf16[128,2560]{1,0:T(8,128)(2,1)S(1)} %bitcast.64), channel_id=1, source_target_pairs={{0,96},{32,0},{64,32},{96,64},{1,97},{33,1},{65,33},{97,65},{2,98}... | collective-permute-start | bytes 1966088 | tf_op jit(solution)/shard_map/ppermute | solution.py:306
  82.0 17.8 %collective-permute-start.1 = (bf16[128,2560]{1,0:T(8,128)(2,1)S(1)}, bf16[128,2560]{1,0:T(8,128)(2,1)S(1)}, u32[]{:S(2)}, u32[]{:S(2)}) collective-permute-start(bf16[128,2560]{1,0:T(8,128)(2,1)S(1)} %bitcast.65), channel_id=1, source_target_pairs={{0,32},{32,64},{64,96},{96,0},{1,33},{33,65},{65,97},{97,1},{2,34}... | collective-permute-start | bytes 1966088 | tf_op jit(solution)/shard_map/ppermute | solution.py:306
  84.1 25.3 %collective-permute-start.8 = (bf16[512,512]{1,0:T(8,128)(2,1)S(1)}, bf16[512,512]{1,0:T(8,128)(2,1)}, u32[]{:S(2)}, u32[]{:S(2)}) collective-permute-start(bf16[512,512]{1,0:T(8,128)(2,1)S(1)} %slice.33), channel_id=1, source_target_pairs={{0,24},{8,0},{16,8},{24,16},{1,25},{9,1},{17,9},{25,17},{2,26},{10... | collective-permute-start | bytes 1572872 | tf_op jit(solution)/shard_map/ppermute | solution.py:306
  87.6 21.7 %collective-permute-start.7 = (bf16[512,512]{1,0:T(8,128)(2,1)S(1)}, bf16[512,512]{1,0:T(8,128)(2,1)}, u32[]{:S(2)}, u32[]{:S(2)}) collective-permute-start(bf16[512,512]{1,0:T(8,128)(2,1)S(1)} %slice.32), channel_id=1, source_target_pairs={{0,8},{8,16},{16,24},{24,0},{1,9},{9,17},{17,25},{25,1},{2,10},{10... | collective-permute-start | bytes 1572872 | tf_op jit(solution)/shard_map/ppermute | solution.py:306
  98.0 11.4 %copy-start.3 = (bf16[128,2560]{1,0:T(8,128)(2,1)}, bf16[128,2560]{1,0:T(8,128)(2,1)S(1)}, u32[]{:S(2)}) copy-start(bf16[128,2560]{1,0:T(8,128)(2,1)S(1)} %collective-permute-done.2.refs_2_) | copy-start | bytes 1966084
  98.0 8.6 %collective-permute-start.4 = (bf16[64,2560]{1,0:T(8,128)(2,1)S(1)}, bf16[64,2560]{1,0:T(8,128)(2,1)S(1)}, u32[]{:S(2)}, u32[]{:S(2)}) collective-permute-start(bf16[64,2560]{1,0:T(8,128)(2,1)S(1)} %slice.31), channel_id=1, source_target_pairs={{0,96},{32,0},{64,32},{96,64},{1,97},{33,1},{65,33},{97,65},{2,98}... | collective-permute-start | bytes 983048 | tf_op jit(solution)/shard_map/ppermute | solution.py:306
  99.8 0.8 copy-start.4
  99.8 9.5 %collective-permute-start.3 = (bf16[64,2560]{1,0:T(8,128)(2,1)S(1)}, bf16[64,2560]{1,0:T(8,128)(2,1)S(1)}, u32[]{:S(2)}, u32[]{:S(2)}) collective-permute-start(bf16[64,2560]{1,0:T(8,128)(2,1)S(1)} %slice.30), channel_id=1, source_target_pairs={{0,32},{32,64},{64,96},{96,0},{1,33},{33,65},{65,97},{97,1},{2,34}... | collective-permute-start | bytes 983048 | tf_op jit(solution)/shard_map/ppermute | solution.py:306
  106.7 2.7 copy-start.8
  109.4 0.7 copy-start.9
  151.7 17.2 %collective-permute-start.11 = (f32[4,5,2,512]{3,2,1,0:T(2,128)}, f32[4,5,2,512]{3,2,1,0:T(2,128)S(1)}, u32[]{:S(2)}, u32[]{:S(2)}) collective-permute-start(f32[4,5,2,512]{3,2,1,0:T(2,128)} %get-tuple-element.9.refs_0_), channel_id=1, source_target_pairs={{0,64},{32,96},{64,0},{96,32},{1,65},{33,97},{65,1},{97,33},{2,66}... | collective-permute-start | bytes 245768 | tf_op jit(solution)/shard_map/ppermute | solution.py:306
  166.8 3.5 %collective-permute-start.10 = (f32[4,5,2,512]{3,2,1,0:T(2,128)}, f32[4,5,2,512]{3,2,1,0:T(2,128)S(1)}, u32[]{:S(2)}, u32[]{:S(2)}) collective-permute-start(f32[4,5,2,512]{3,2,1,0:T(2,128)} %get-tuple-element.9.refs_0_), channel_id=1, source_target_pairs={{0,96},{32,0},{64,32},{96,64},{1,97},{33,1},{65,33},{97,65},{2,98}... | collective-permute-start | bytes 245768 | tf_op jit(solution)/shard_map/ppermute | solution.py:306
  166.8 4.7 %collective-permute-start.9 = (f32[4,5,2,512]{3,2,1,0:T(2,128)}, f32[4,5,2,512]{3,2,1,0:T(2,128)S(1)}, u32[]{:S(2)}, u32[]{:S(2)}) collective-permute-start(f32[4,5,2,512]{3,2,1,0:T(2,128)} %get-tuple-element.9.refs_0_), channel_id=1, source_target_pairs={{0,32},{32,64},{64,96},{96,0},{1,33},{33,65},{65,97},{97,1},{2,34}... | collective-permute-start | bytes 245768 | tf_op jit(solution)/shard_map/ppermute | solution.py:306
  168.8 2.7 copy-start.5
  170.3 1.2 copy-start.6
  171.5 0.6 copy-start.7
  193.3 42.0 %copy-start.10 = (u32[128]{0:T(128)S(1)}, u32[128]{0:T(128)}, u32[]{:S(2)}) copy-start(u32[128]{0:T(128)} %constant.80) | copy-start | bytes 1540
  194.9 53.5 %all-to-all-start = ((f32[64,2,8,128]{3,2,1,0:T(8,128)}), f32[64,2,8,128]{3,2,1,0:T(8,128)S(1)}, u32[]{:S(2)}, u32[]{:S(2)}) async-start(f32[64,2,8,128]{3,2,1,0:T(8,128)} %broadcast_in_dim.2), calls=%async_computation | async-start | bytes 1048576 | tf_op jit(solution)/shard_map/all_to_all | solution.py:349
  248.4 0.8 copy-start
Sparse Core Ops, SparseCore 0:
  30.3 50.5 all-gather.4
